TPU v7x, 32 devices: a whole 2x2x4 slice. The times are simulated.
32 devices in a mesh: gx: 8 (over y, x, core), gz: 4 (over z).
Axes of the slice: x: 2, y: 2, z: 4, core: 2. Of those that a mesh axis runs over, the one named last changes fastest.
Arguments:
- adjoint: float32 [3, 128, 128, 512], P(None, 'gx', None, 'gz'), may hold values from -6 to 6
- velocity: float32 [3, 128, 128, 512], P(None, 'gx', None, 'gz'), may hold values from -0.45 to 0.45
- viscosity: float32 [128, 128, 512], P('gx', None, 'gz'), may hold values from 0.02 to 0.15
- filters: bfloat16 [128, 512, 512], P(('gx', 'gz')), may hold values from -0.25 to 0.25
- block_tiles: int32 [128, 8], replicated, may hold values from 0 to 127, all different within a row
- tile_place: int32 [128], replicated, may hold values from 0 to 127, each once
Outputs:
- adjoint_out: float32 [3, 128, 128, 512], P(None, 'gx', None, 'gz')
- generator_tile_gradient: float32 [128, 3, 512], P(('gx', 'gz'))
Inputs may be any that keep to these rules, and one draw needn't show every extreme that they name: `block_tiles`: each row lists 8 different tiles; every tile is listed by some block. `tile_place`: each tile exactly once.
All inputs are finite; a program needn't handle non-finite values.
Results may differ from a plain program's by a relative error of at most 0.0003.
Values sent between devices are 32-bit elements; how exact they have to be, the bound alone decides.
A program may use at most 192 MiB of HBM per device.

v0:
```python
import jax
import jax.numpy as jnp
from jax import lax
from jax.sharding import PartitionSpec as P

BY = 4
BZ = 128


def with_halo(block, sides, width, periodic):
    for axis, dim in sides:
        count = lax.axis_size(axis)
        forward = [(i, i + 1) for i in range(count - 1)]
        if periodic:
            forward.append((count - 1, 0))
        backward = [(target, source) for source, target in forward]
        low = lax.ppermute(
            lax.slice_in_dim(block, block.shape[dim] - width, None, axis=dim), axis, forward
        )
        high = lax.ppermute(lax.slice_in_dim(block, 0, width, axis=dim), axis, backward)
        block = jnp.concatenate([low, block, high], axis=dim)
    return block


def advance(padded, visc_pad, velocity):
    centre = padded[..., 1:-1, 1:-1, 1:-1]
    east_cell = padded[..., 2:, 1:-1, 1:-1]
    west_cell = padded[..., :-2, 1:-1, 1:-1]
    north_cell = padded[..., 1:-1, 2:, 1:-1]
    south_cell = padded[..., 1:-1, :-2, 1:-1]
    upper_cell = padded[..., 1:-1, 1:-1, 2:]
    lower_cell = padded[..., 1:-1, 1:-1, :-2]
    visc_mid = visc_pad[1:-1, 1:-1, 1:-1]
    east_face = 0.5 * (visc_mid + visc_pad[2:, 1:-1, 1:-1])
    west_face = 0.5 * (visc_mid + visc_pad[:-2, 1:-1, 1:-1])
    north_face = 0.5 * (visc_mid + visc_pad[1:-1, 2:, 1:-1])
    south_face = 0.5 * (visc_mid + visc_pad[1:-1, :-2, 1:-1])
    upper_face = 0.5 * (visc_mid + visc_pad[1:-1, 1:-1, 2:])
    lower_face = 0.5 * (visc_mid + visc_pad[1:-1, 1:-1, :-2])
    transport = 0.5 * (
        velocity[0] * (east_cell - west_cell)
        + velocity[1] * (north_cell - south_cell)
        + velocity[2] * (upper_cell - lower_cell)
    )
    diffusion = east_face * (east_cell - centre) - west_face * (centre - west_cell)
    diffusion = diffusion + north_face * (north_cell - centre) - south_face * (centre - south_cell)
    diffusion = diffusion + upper_face * (upper_cell - centre) - lower_face * (centre - lower_cell)
    return centre + transport + diffusion


def widened_state(field, width):
    along_x = with_halo(field, (("gx", 1),), width, False)
    return with_halo(along_x, (("gz", 3),), width, True)


def widen_coef(field, width):
    along_x = with_halo(field, (("gx", 1),), width, False)
    return with_halo(along_x, (("gz", 3),), width, True)


def wall_pad(field):
    return jnp.pad(field, ((0, 0),) * (field.ndim - 2) + ((1, 1), (0, 0)))


def cut_blocks(face, group_list):
    comps, rows_all, cols_all = face.shape
    reshaped_array = face.reshape(
        comps, rows_all // BY, BY, group_list, cols_all // (group_list * BZ), BZ
    )
    return reshaped_array.transpose(3, 1, 4, 0, 2, 5).reshape(-1, comps * BY * BZ)


def place_of(lists, tile_place):
    tile_count = tile_place.shape[0]
    matches = lists[:, :, None] == jnp.arange(tile_count, dtype=jnp.int32)[None, None, :]
    return jnp.sum(jnp.where(matches, tile_place[None, None, :], 0), axis=2)


def table_rows(places, blocks, row_count):
    wanted = jnp.arange(row_count, dtype=jnp.int32)
    onehot = jnp.sum((places[None, :, :] == wanted[:, None, None]).astype(jnp.float32), axis=2)
    return jnp.dot(
        onehot, blocks, precision=lax.Precision.HIGHEST, preferred_element_type=jnp.float32
    )


def shards(adjoint, velocity, viscosity, filters, block_tiles, tile_place):
    global_streamwise_index = lax.axis_index("gx")
    gz_index = lax.axis_index("gz")
    visc_pad = wall_pad(widen_coef(viscosity[None], 1)[0])
    state = adjoint
    for step_index in range(2):
        state = advance(wall_pad(widened_state(state, 1)), visc_pad, velocity)
    face = state[:, 0]
    column_blocks = block_tiles.shape[0] // lax.axis_size("gz")
    tile_rows = filters.shape[0]
    blocks = cut_blocks(face, 1) * (global_streamwise_index == 0).astype(jnp.float32)
    lists = lax.dynamic_slice_in_dim(block_tiles, gz_index * column_blocks, column_blocks, 0)
    places = place_of(lists, tile_place)
    sums = lax.psum_scatter(
        table_rows(places, blocks, tile_rows * lax.axis_size(("gx", "gz"))),
        ("gx", "gz"),
        scatter_dimension=0,
        tiled=True,
    )
    tile_view = sums.reshape(tile_rows, 3, -1)
    generator_tile_gradient = jnp.einsum(
        "gvl,gls->gvs",
        tile_view,
        filters.astype(jnp.float32),
        precision=lax.Precision.HIGHEST,
        preferred_element_type=jnp.float32,
    )
    return (state, generator_tile_gradient)


def solution(mesh):
    placed = (
        P(None, "gx", None, "gz"),
        P(None, "gx", None, "gz"),
        P("gx", None, "gz"),
        P(("gx", "gz"), None, None),
        P(),
        P(),
    )
    return jax.shard_map(
        shards,
        mesh=mesh,
        in_specs=placed,
        out_specs=(P(None, "gx", None, "gz"), P(("gx", "gz"), None, None)),
        check_vma=False,
    )
```

profile of v0, /device:TPU:0, one launch (start us, length us, event | category | flops | bytes accessed | tf_op | source)
XLA Modules:
  0.0 313.9 jit_solution(11689441566400433122)
XLA Ops:
  7.2 1.7 copy.89
  9.0 2.4 collective-permute-start.4
  11.3 1.3 collective-permute-start.5
  12.6 1.8 fusion.46
  14.5 5.1 %collective-permute-start.1 = (f32[3,1,128,128]{3,2,0,1:T(8,128)}, f32[3,1,128,128]{3,2,0,1:T(8,128)S(1)}, u32[]{:S(2)}, u32[]{:S(2)}) collective-permute-start(f32[3,1,128,128]{3,2,0,1:T(8,128)} %get-tuple-element.22), channel_id=1, source_target_pairs={{0,4},{4,8},{8,12},{12,16},{16,20},{20,24},{24,28},{1,5},{5,9},{9,... | collective-permute-start | bytes 589832 | tf_op jit(solution)/shard_map/ppermute | solution.py:17
  19.6 1.3 collective-permute-start
  21.0 1.6 collective-permute-start.6
  22.6 2.2 collective-permute-start.7
  24.8 3.6 %slice_bitcast_fusion.2 = (f32[16,128,128]{2,1,0:T(8,128)}, f32[16,128,128]{2,1,0:T(8,128)}, f32[16,128,128]{2,1,0:T(8,128)}) fusion(f32[3,16,128,128]{3,2,1,0:T(8,128)} %param.7), kind=kLoop, calls=%fused_computation.71 | loop fusion | bytes 6291456 | tf_op jit(solution)/shard_map/mul | solution.py:41
  28.4 1.9 copy.88
  30.9 1.4 maximum_bitcast_fusion
  32.3 2.1 constant_dynamic-update-slice_fusion.1
  34.5 0.9 constant_dynamic-update-slice_fusion
  35.4 4.1 %fusion.44 = (f32[3,18,128,1]{3,2,0,1:T(8,128)}, f32[3,18,128,1]{3,2,0,1:T(8,128)}) fusion(f32[3,18,128,128]{3,2,0,1:T(8,128)S(1)} %constant_dynamic-update-slice_fusion), kind=kLoop, calls=%fused_computation.88 | loop fusion | bytes 110592 | tf_op jit(solution)/shard_map/slice | solution.py:18
  39.5 4.1 %copy.82 = f32[3,18,128,1]{2,1,3,0:T(8,128)} copy(f32[3,18,128,1]{3,2,0,1:T(8,128)} %get-tuple-element.14) | data formatting | bytes 55296 | tf_op jit(solution)/shard_map/slice | solution.py:18
  43.6 4.1 %copy.83 = f32[3,18,128,1]{2,1,3,0:T(8,128)} copy(f32[3,18,128,1]{3,2,0,1:T(8,128)} %get-tuple-element.15) | data formatting | bytes 55296 | tf_op jit(solution)/shard_map/slice | solution.py:20
  47.7 3.8 %collective-permute-start.3 = (f32[3,18,128,1]{2,1,3,0:T(8,128)}, f32[3,18,128,1]{2,1,3,0:T(8,128)}, u32[]{:S(2)}, u32[]{:S(2)}) collective-permute-start(f32[3,18,128,1]{2,1,3,0:T(8,128)} %copy.83), channel_id=1, source_target_pairs={{1,0},{2,1},{3,2},{0,3},{5,4},{6,5},{7,6},{4,7},{9,8},{10,9},{11,1... | collective-permute-start | bytes 82952 | tf_op jit(solution)/shard_map/ppermute | solution.py:20
  51.6 3.5 %fusion.40 = (f32[16,128,128]{1,2,0:T(8,128)}, f32[16,128,128]{1,2,0:T(8,128)}, f32[16,128,128]{1,2,0:T(8,128)}, f32[16,128,128]{1,2,0:T(8,128)}, f32[16,128,128]{1,2,0:T(8,128)}, /*index=5*/f32[16,128,128]{1,2,0:T(8,128)}) fusion(f32[18,128,130]{1,2,0:T(8,128)S(1)} %maximum_bitcast_fusion), kind=kLoop, calls=%fused_computation.68 | loop fusion | flops 3145728 | bytes 12787712 | tf_op jit(solution)/shard_map/mul | solution.py:34
  55.1 1.6 copy.100
  56.6 2.7 copy.90
  59.3 2.5 copy.92
  61.8 2.5 copy.94
  64.4 2.5 copy.96
  66.9 2.6 copy.98
  69.5 3.3 %copy.84 = f32[3,18,128,1]{3,2,0,1:T(8,128)} copy(f32[3,18,128,1]{2,1,3,0:T(8,128)} %collective-permute-done.2) | data formatting | bytes 55296 | tf_op jit(solution)/shard_map/ppermute | solution.py:17
  72.8 3.2 %copy.85 = f32[3,18,128,1]{3,2,0,1:T(8,128)} copy(f32[3,18,128,1]{2,1,3,0:T(8,128)} %collective-permute-done.3) | data formatting | bytes 55296 | tf_op jit(solution)/shard_map/ppermute | solution.py:20
  76.0 8.0 %select_maximum_fusion.4 = f32[3,18,130,130]{3,2,0,1:T(8,128)} fusion(f32[3,18,128,1]{3,2,0,1:T(8,128)} %copy.85, f32[3,18,128,128]{3,2,0,1:T(8,128)} %copy-done.1, f32[3,18,128,1]{3,2,0,1:T(8,128)} %copy.84), kind=kLoop, calls=%fused_computation.6 | loop fusion | flops 7300800 | bytes 7244640 | tf_op jit(solution)/shard_map/concatenate | solution.py:21
  83.9 19.1 %fusion.25 = f32[3,16,128,128]{3,2,0,1:T(8,128)} fusion(f32[3,16,128,128]{3,2,0,1:T(8,128)} %copy.88, f32[3,1,128,128]{3,2,0,1:T(8,128)S(1)} %collective-permute-done.1, f32[3,1,128,128]{3,2,0,1:T(8,128)} %collective-permute-done, f32[3,18,128,1]{3,2,0,1:T(8,128)} %copy.85, f32[3,18,128,128]{3,2,0,1:T(8,128)} %copy-done.1, f32[3,18,128,1]{3,2,0,1:T(8,128)} %copy.84, ...), kind=kLoop, calls=%fused_computation.45 | loop fusion | flops 25165824 | bytes 26007552 | tf_op jit(solution)/shard_map/add | solution.py:48
  103.1 1.8 fusion.45
  104.9 1.3 collective-permute-start.8
  106.2 3.9 %collective-permute-start.9 = (f32[3,1,128,128]{3,2,0,1:T(8,128)}, f32[3,1,128,128]{3,2,0,1:T(8,128)S(1)}, u32[]{:S(2)}, u32[]{:S(2)}) collective-permute-start(f32[3,1,128,128]{3,2,0,1:T(8,128)} %get-tuple-element.17), channel_id=1, source_target_pairs={{0,4},{4,8},{8,12},{12,16},{16,20},{20,24},{24,28},{1,5},{5,9},{9,... | collective-permute-start | bytes 589832 | tf_op jit(solution)/shard_map/ppermute | solution.py:17
  111.5 1.9 select_reduce_fusion
  113.5 2.1 pad_maximum_fusion
  115.6 4.1 %fusion.43 = (f32[3,18,128,1]{3,2,0,1:T(8,128)}, f32[3,18,128,1]{3,2,0,1:T(8,128)}) fusion(f32[3,18,128,128]{3,2,0,1:T(8,128)S(1)} %pad_maximum_fusion), kind=kLoop, calls=%fused_computation.87 | loop fusion | bytes 110592 | tf_op jit(solution)/shard_map/slice | solution.py:18
  119.7 4.1 %copy.102 = f32[3,18,128,1]{2,1,3,0:T(8,128)} copy(f32[3,18,128,1]{3,2,0,1:T(8,128)} %get-tuple-element.12) | data formatting | bytes 55296 | tf_op jit(solution)/shard_map/slice | solution.py:18
  123.8 4.1 %copy.103 = f32[3,18,128,1]{2,1,3,0:T(8,128)} copy(f32[3,18,128,1]{3,2,0,1:T(8,128)} %get-tuple-element.13) | data formatting | bytes 55296 | tf_op jit(solution)/shard_map/slice | solution.py:20
  127.9 3.8 %collective-permute-start.11 = (f32[3,18,128,1]{2,1,3,0:T(8,128)}, f32[3,18,128,1]{2,1,3,0:T(8,128)}, u32[]{:S(2)}, u32[]{:S(2)}) collective-permute-start(f32[3,18,128,1]{2,1,3,0:T(8,128)} %copy.103), channel_id=1, source_target_pairs={{1,0},{2,1},{3,2},{0,3},{5,4},{6,5},{7,6},{4,7},{9,8},{10,9},{11,1... | collective-permute-start | bytes 82952 | tf_op jit(solution)/shard_map/ppermute | solution.py:20
  131.8 0.8 convert_reduce_fusion
  132.6 3.3 %copy.104 = f32[3,18,128,1]{3,2,0,1:T(8,128)} copy(f32[3,18,128,1]{2,1,3,0:T(8,128)} %collective-permute-done.10) | data formatting | bytes 55296 | tf_op jit(solution)/shard_map/ppermute | solution.py:17
  135.9 3.3 %copy.105 = f32[3,18,128,1]{3,2,0,1:T(8,128)} copy(f32[3,18,128,1]{2,1,3,0:T(8,128)} %collective-permute-done.11) | data formatting | bytes 55296 | tf_op jit(solution)/shard_map/ppermute | solution.py:20
  139.2 10.1 %select_maximum_fusion = f32[3,18,130,130]{3,2,0,1:T(8,128)} fusion(f32[3,18,128,1]{3,2,0,1:T(8,128)} %copy.105, f32[3,18,128,1]{3,2,0,1:T(8,128)} %copy.104, f32[3,1,128,128]{3,2,0,1:T(8,128)S(1)} %collective-permute-done.8, f32[3,16,128,128]{3,2,0,1:T(8,128)} %fusion.25, f32[3,1,128,128]{3,2,0,1:T(8,128)S(1)} %collective-permute-done.9), kind=kLoop, calls=%fused_computation.2 | loop fusion | flops 10951200 | bytes 7244640 | tf_op jit(solution)/shard_map/concatenate | solution.py:21
  149.4 19.0 %fusion.9 = f32[3,16,128,128]{3,2,0,1:T(8,128)} fusion(f32[3,16,128,128]{3,2,0,1:T(8,128)} %fusion.25, f32[3,1,128,128]{3,2,0,1:T(8,128)S(1)} %collective-permute-done.9, f32[3,1,128,128]{3,2,0,1:T(8,128)S(1)} %collective-permute-done.8, f32[3,18,128,1]{3,2,0,1:T(8,128)} %copy.105, f32[3,18,128,1]{3,2,0,1:T(8,128)} %copy.104, ...), kind=kLoop, calls=%fused_computation.25 | loop fusion | flops 28311552 | bytes 22468608 | tf_op jit(solution)/shard_map/add | solution.py:48
  168.4 0.9 slice_multiply_fusion
  169.5 1.7 fusion.48
  171.2 3.9 %copy.111 = f32[3,16,128,128]{3,2,1,0:T(8,128)} copy(f32[3,16,128,128]{3,2,0,1:T(8,128)} %fusion.9) | data formatting | bytes 6291456
  175.2 129.6 %all-reduce.6.cloned.1.call-done = f32[128,1536]{1,0:T(8,128)} async-done(((f32[128,1536]{1,0:T(8,128)}), f32[128,1536]{1,0:T(8,128)}) %all-reduce.6.cloned.1.call-update) | async-done | bytes 786448
  304.7 0.8 constant_dynamic-slice_fusion
  305.5 0.9 fusion.41
  (40 shorter events, 3.0 us)
Async XLA Ops:
  7.2 298.4 %copy-start = (bf16[4,512,512]{2,1,0:T(8,128)(2,1)S(1)}, bf16[4,512,512]{2,1,0:T(8,128)(2,1)}, u32[]{:S(2)}) copy-start(bf16[4,512,512]{2,1,0:T(8,128)(2,1)} %param.9) | copy-start | bytes 6291460
  7.2 297.5 %all-reduce.6.cloned.1.call-start = ((), (), s32[]{:S(2)}) async-start(), calls=%async_computation | async-start | bytes 1572864
  8.9 19.5 %copy-start.3 = (f32[16,128,128]{1,2,0:T(8,128)}, f32[16,128,128]{1,2,0:T(8,128)S(1)}, u32[]{:S(2)}) copy-start(f32[16,128,128]{1,2,0:T(8,128)S(1)} %copy.89) | copy-start | bytes 3145732
  9.0 11.9 %collective-permute-start.4 = (f32[1,1,128,128]{2,3,1,0:T(8,128)S(1)}, f32[1,1,128,128]{2,3,1,0:T(8,128)S(1)}, u32[]{:S(2)}, u32[]{:S(2)}) collective-permute-start(f32[1,1,128,128]{2,3,1,0:T(8,128)S(1)} %get-tuple-element.31), channel_id=1, source_target_pairs={{0,4},{4,8},{8,12},{12,16},{16,20},{20,24},{24,28},{1,5},{5,9},{9,... | collective-permute-start | bytes 196616 | tf_op jit(solution)/shard_map/ppermute | solution.py:17
  11.3 9.6 %collective-permute-start.5 = (f32[1,1,128,128]{2,3,1,0:T(8,128)S(1)}, f32[1,1,128,128]{2,3,1,0:T(8,128)S(1)}, u32[]{:S(2)}, u32[]{:S(2)}) collective-permute-start(f32[1,1,128,128]{2,3,1,0:T(8,128)S(1)} %get-tuple-element.32), channel_id=1, source_target_pairs={{4,0},{8,4},{12,8},{16,12},{20,16},{24,20},{28,24},{5,1},{9,5},{13... | collective-permute-start | bytes 196616 | tf_op jit(solution)/shard_map/ppermute | solution.py:20
  14.5 17.9 %collective-permute-start.1 = (f32[3,1,128,128]{3,2,0,1:T(8,128)}, f32[3,1,128,128]{3,2,0,1:T(8,128)S(1)}, u32[]{:S(2)}, u32[]{:S(2)}) collective-permute-start(f32[3,1,128,128]{3,2,0,1:T(8,128)} %get-tuple-element.22), channel_id=1, source_target_pairs={{0,4},{4,8},{8,12},{12,16},{16,20},{20,24},{24,28},{1,5},{5,9},{9,... | collective-permute-start | bytes 589832 | tf_op jit(solution)/shard_map/ppermute | solution.py:17
  19.6 14.9 %collective-permute-start = (f32[3,1,128,128]{3,2,0,1:T(8,128)}, f32[3,1,128,128]{3,2,0,1:T(8,128)}, u32[]{:S(2)}, u32[]{:S(2)}) collective-permute-start(f32[3,1,128,128]{3,2,0,1:T(8,128)} %get-tuple-element.21), channel_id=1, source_target_pairs={{4,0},{8,4},{12,8},{16,12},{20,16},{24,20},{28,24},{5,1},{9,5},{13... | collective-permute-start | bytes 589832 | tf_op jit(solution)/shard_map/ppermute | solution.py:20
  20.9 7.5 %copy-start.4 = (f32[1,1,128,128]{2,3,1,0:T(8,128)}, f32[1,1,128,128]{2,3,1,0:T(8,128)S(1)}, u32[]{:S(2)}) copy-start(f32[1,1,128,128]{2,3,1,0:T(8,128)S(1)} %collective-permute-done.4) | copy-start | bytes 196612
  20.9 7.5 %copy-start.5 = (f32[1,1,128,128]{2,3,1,0:T(8,128)}, f32[1,1,128,128]{2,3,1,0:T(8,128)S(1)}, u32[]{:S(2)}) copy-start(f32[1,1,128,128]{2,3,1,0:T(8,128)S(1)} %collective-permute-done.5) | copy-start | bytes 196612
  21.0 9.4 %collective-permute-start.6 = (f32[1,18,128,1]{2,3,1,0:T(1,128)S(1)}, f32[1,18,128,1]{2,3,1,0:T(1,128)S(1)}, u32[]{:S(2)}, u32[]{:S(2)}) collective-permute-start(f32[1,18,128,1]{2,3,1,0:T(1,128)S(1)} %get-tuple-element.29), channel_id=1, source_target_pairs={{0,1},{1,2},{2,3},{3,0},{4,5},{5,6},{6,7},{7,4},{8,9},{9,10},{10,1... | collective-permute-start | bytes 27656 | tf_op jit(solution)/shard_map/ppermute | solution.py:17
  22.6 5.9 %copy-start.2 = (f32[3,16,128,128]{3,2,1,0:T(8,128)S(1)}, f32[3,16,128,128]{3,2,1,0:T(8,128)}, u32[]{:S(2)}) copy-start(f32[3,16,128,128]{3,2,1,0:T(8,128)} %param.6) | copy-start | bytes 9437188
  22.6 8.3 %collective-permute-start.7 = (f32[1,18,128,1]{2,3,1,0:T(1,128)S(1)}, f32[1,18,128,1]{2,3,1,0:T(1,128)}, u32[]{:S(2)}, u32[]{:S(2)}) collective-permute-start(f32[1,18,128,1]{2,3,1,0:T(1,128)S(1)} %get-tuple-element.30), channel_id=1, source_target_pairs={{1,0},{2,1},{3,2},{0,3},{5,4},{6,5},{7,6},{4,7},{9,8},{10,9},{11,1... | collective-permute-start | bytes 27656 | tf_op jit(solution)/shard_map/ppermute | solution.py:20
  30.3 0.6 copy-start.6
  35.4 4.1 %copy-start.1 = (f32[3,18,128,128]{3,2,0,1:T(8,128)}, f32[3,18,128,128]{3,2,0,1:T(8,128)S(1)}, u32[]{:S(2)}) copy-start(f32[3,18,128,128]{3,2,0,1:T(8,128)S(1)} %constant_dynamic-update-slice_fusion) | copy-start | bytes 10616836
  43.6 25.8 %collective-permute-start.2 = (f32[3,18,128,1]{2,1,3,0:T(8,128)}, f32[3,18,128,1]{2,1,3,0:T(8,128)}, u32[]{:S(2)}, u32[]{:S(2)}) collective-permute-start(f32[3,18,128,1]{2,1,3,0:T(8,128)} %copy.82), channel_id=1, source_target_pairs={{0,1},{1,2},{2,3},{3,0},{4,5},{5,6},{6,7},{7,4},{8,9},{9,10},{10,1... | collective-permute-start | bytes 82952 | tf_op jit(solution)/shard_map/ppermute | solution.py:17
  47.7 25.1 %collective-permute-start.3 = (f32[3,18,128,1]{2,1,3,0:T(8,128)}, f32[3,18,128,1]{2,1,3,0:T(8,128)}, u32[]{:S(2)}, u32[]{:S(2)}) collective-permute-start(f32[3,18,128,1]{2,1,3,0:T(8,128)} %copy.83), channel_id=1, source_target_pairs={{1,0},{2,1},{3,2},{0,3},{5,4},{6,5},{7,6},{4,7},{9,8},{10,9},{11,1... | collective-permute-start | bytes 82952 | tf_op jit(solution)/shard_map/ppermute | solution.py:20
  83.9 26.2 %copy-start.7 = (s32[128,8]{0,1:T(8,128)S(1)}, s32[128,8]{0,1:T(8,128)}, u32[]{:S(2)}) copy-start(s32[128,8]{0,1:T(8,128)} %param.10) | copy-start | bytes 12292
  104.9 8.6 %collective-permute-start.8 = (f32[3,1,128,128]{3,2,0,1:T(8,128)}, f32[3,1,128,128]{3,2,0,1:T(8,128)S(1)}, u32[]{:S(2)}, u32[]{:S(2)}) collective-permute-start(f32[3,1,128,128]{3,2,0,1:T(8,128)} %get-tuple-element.16), channel_id=1, source_target_pairs={{4,0},{8,4},{12,8},{16,12},{20,16},{24,20},{28,24},{5,1},{9,5},{13... | collective-permute-start | bytes 589832 | tf_op jit(solution)/shard_map/ppermute | solution.py:20
  106.2 7.3 %collective-permute-start.9 = (f32[3,1,128,128]{3,2,0,1:T(8,128)}, f32[3,1,128,128]{3,2,0,1:T(8,128)S(1)}, u32[]{:S(2)}, u32[]{:S(2)}) collective-permute-start(f32[3,1,128,128]{3,2,0,1:T(8,128)} %get-tuple-element.17), channel_id=1, source_target_pairs={{0,4},{4,8},{8,12},{12,16},{16,20},{20,24},{24,28},{1,5},{5,9},{9,... | collective-permute-start | bytes 589832 | tf_op jit(solution)/shard_map/ppermute | solution.py:17
  123.8 8.8 %collective-permute-start.10 = (f32[3,18,128,1]{2,1,3,0:T(8,128)}, f32[3,18,128,1]{2,1,3,0:T(8,128)}, u32[]{:S(2)}, u32[]{:S(2)}) collective-permute-start(f32[3,18,128,1]{2,1,3,0:T(8,128)} %copy.102), channel_id=1, source_target_pairs={{0,1},{1,2},{2,3},{3,0},{4,5},{5,6},{6,7},{7,4},{8,9},{9,10},{10,1... | collective-permute-start | bytes 82952 | tf_op jit(solution)/shard_map/ppermute | solution.py:17
  127.9 8.0 %collective-permute-start.11 = (f32[3,18,128,1]{2,1,3,0:T(8,128)}, f32[3,18,128,1]{2,1,3,0:T(8,128)}, u32[]{:S(2)}, u32[]{:S(2)}) collective-permute-start(f32[3,18,128,1]{2,1,3,0:T(8,128)} %copy.103), channel_id=1, source_target_pairs={{1,0},{2,1},{3,2},{0,3},{5,4},{6,5},{7,6},{4,7},{9,8},{10,9},{11,1... | collective-permute-start | bytes 82952 | tf_op jit(solution)/shard_map/ppermute | solution.py:20
Sparse Core Ops, SparseCore 0:
  171.4 133.3 all-reduce.5
where the time goes:
time: 315 us; the launch traced here: 314 us
  waiting for transfers between devices  130 us (41%)
  local copies, waits for them, and re-layouts  73.5 us (23%)
  other arithmetic  67 us (21%)
  starting transfers between devices  26.8 us (9%)
  between operations  14.3 us (5%)
    unnamed x2, waiting for transfers between devices  130 us
    add x2, other arithmetic, advance(): return centre + transport + diffusion  38.2 us
    concatenate x3, other arithmetic, with_halo(): block = jnp.concatenate([low, block, high], axis=dim)  20.2 us
    slice x5, local copies, waits for them, and re-layouts, with_halo(): lax.slice_in_dim(block, block.shape[dim] - width, None, axis=dim)  16.4 us
    ppermute x6, starting transfers between devices, with_halo(): lax.ppermute(lax.slice_in_dim(block, 0, width, axis=dim), axis, backward)  13.7 us
    ppermute x6, starting transfers between devices, with_halo(): lax.ppermute(lax.slice_in_dim(block, block.shape[dim] - width, None, axis...  13 us
    slice x4, local copies, waits for them, and re-layouts, with_halo(): lax.slice_in_dim(block, 0, width, axis=dim)  11.8 us
    unnamed x23, local copies, waits for them, and re-layouts  11.7 us
  transfers between devices with their start and end apart: 13, of which 1 were waited for; matrix products, arithmetic and copies ran while one was open for 16% of the time, Pallas kernels for 0%

commit v1 on v0

v1 whole, which is shorter than its diff:
```python
import functools

import jax
import jax.numpy as jnp
from jax import lax
from jax.experimental import pallas as pl
from jax.experimental.pallas import tpu as pltpu
from jax.sharding import PartitionSpec as P

BY = 4
PAD = 8
MESH = pl.DeviceIdType.MESH


def split_parts(value):
    high = value.astype(jnp.bfloat16)
    low = (value - high.astype(jnp.float32)).astype(jnp.bfloat16)
    return high, low


def kernel(
    gxn, gzn, chunk,
    adj_hbm, vel_hbm, visc_hbm, filt_hbm, lists_ref, place_ref,
    out_hbm, grad_ref,
    lam, mid, visc, vel, filt, coef, out, pack, take, joined, gate, contrib, got, left_side,
    load_sem, store_sem, x_send, x_recv, z_send, z_recv, t_send, t_recv,
):
    comps, nx, ny, nz = adj_hbm.shape
    tiles = place_ref.shape[1]
    tile_rows = filt_hbm.shape[0]
    half = nx // 2
    gx = lax.axis_index("gx")
    gz = lax.axis_index("gz")
    upper = lax.rem(gz + 1, gzn)
    lower = lax.rem(gz + gzn - 1, gzn)
    me = gx * gzn + gz
    rows = pl.ds(PAD, ny)
    f32 = jnp.float32

    inner = pl.ds(1, nx)
    loads = [
        pltpu.make_async_copy(adj_hbm, lam.at[:, inner, rows, :], load_sem.at[0]),
        pltpu.make_async_copy(visc_hbm, visc.at[inner, rows, :], load_sem.at[1]),
        pltpu.make_async_copy(vel_hbm, vel, load_sem.at[2]),
        pltpu.make_async_copy(filt_hbm, filt, load_sem.at[3]),
    ]
    for load in loads:
        load.start()

    barrier = pltpu.get_barrier_semaphore()

    def greet(x, z):
        pl.semaphore_signal(barrier, inc=1, device_id=(x, z), device_id_type=MESH)

    greet(gx, upper)
    greet(gx, lower)

    @pl.when(gx < gxn - 1)
    def _():
        greet(gx + 1, gz)

    @pl.when(gx > 0)
    def _():
        greet(gx - 1, gz)

    for z in range(gzn):
        known = (z == gz) | (z == upper) | (z == lower)

        @pl.when(((gx == 0) & jnp.logical_not(known)) | ((gx == 1) & (z != gz)) | (gx > 1))
        def _():
            greet(0, z)

    @pl.when(gx == 0)
    def _():
        pl.semaphore_wait(barrier, gxn * gzn - 1)

    @pl.when((gx > 0) & (gx < gxn - 1))
    def _():
        pl.semaphore_wait(barrier, 4)

    @pl.when((gx > 0) & (gx == gxn - 1))
    def _():
        pl.semaphore_wait(barrier, 3)

    def layers(source, target, plane_dim, slot):
        def plane_of(ref, at, padded):
            index = (slice(None),) * plane_dim + (at,)
            return ref.at[index + ((rows, slice(None)) if padded else ())]

        down = pltpu.make_async_remote_copy(
            plane_of(source[0], source[1], source[3]), plane_of(target, nx + 1, True),
            x_send.at[slot], x_recv.at[slot], device_id=(gx - 1, gz), device_id_type=MESH)
        up = pltpu.make_async_remote_copy(
            plane_of(source[0], source[2], source[3]), plane_of(target, 0, True),
            x_send.at[slot + 1], x_recv.at[slot + 1], device_id=(gx + 1, gz), device_id_type=MESH)
        return down, up

    def start_layers(pair):
        @pl.when(gx > 0)
        def _():
            pair[0].start()

        @pl.when(gx < gxn - 1)
        def _():
            pair[1].start()

    def await_layers(pair):
        @pl.when(gx < gxn - 1)
        def _():
            pair[0].wait_recv()

        @pl.when(gx > 0)
        def _():
            pair[1].wait_recv()

    def await_sent(pair):
        @pl.when(gx > 0)
        def _():
            pair[0].wait_send()

        @pl.when(gx < gxn - 1)
        def _():
            pair[1].wait_send()

    visc_layers = layers((visc_hbm, 0, nx - 1, False), visc, 0, 0)
    lam_layers = layers((adj_hbm, 0, nx - 1, False), lam, 1, 2)
    mid_layers = layers((mid, 1, nx, True), mid, 1, 4)
    start_layers(visc_layers)
    start_layers(lam_layers)

    for ref in (lam, mid):
        ref[:, :, 0:PAD, :] = jnp.zeros((comps, nx + 2, PAD, nz), f32)
        ref[:, :, PAD + ny:, :] = jnp.zeros((comps, nx + 2, PAD, nz), f32)
    visc[:, 0:PAD, :] = jnp.zeros((nx + 2, PAD, nz), f32)
    visc[:, PAD + ny:, :] = jnp.zeros((nx + 2, PAD, nz), f32)
    pack[...] = jnp.zeros_like(pack)

    @pl.when(gx == 0)
    def _():
        lam[:, 0, rows, :] = jnp.zeros((comps, ny, nz), f32)
        mid[:, 0, rows, :] = jnp.zeros((comps, ny, nz), f32)
        visc[0, rows, :] = jnp.zeros((ny, nz), f32)

    @pl.when(gx == gxn - 1)
    def _():
        lam[:, nx + 1, rows, :] = jnp.zeros((comps, ny, nz), f32)
        mid[:, nx + 1, rows, :] = jnp.zeros((comps, ny, nz), f32)
        visc[nx + 1, rows, :] = jnp.zeros((ny, nz), f32)

    lane = lax.broadcasted_iota(jnp.int32, (chunk, nz), 1)
    pair_of = lax.rem(lane + 1, nz) // 2

    def columns(slot):
        to_upper = pltpu.make_async_remote_copy(
            pack.at[slot], take.at[slot, 0], z_send.at[2 * slot], z_recv.at[2 * slot],
            device_id=(gx, upper), device_id_type=MESH)
        to_lower = pltpu.make_async_remote_copy(
            pack.at[slot], take.at[slot, 1], z_send.at[2 * slot + 1], z_recv.at[2 * slot + 1],
            device_id=(gx, lower), device_id_type=MESH)
        return to_upper, to_lower

    def join(slot):
        for copy in columns(slot):
            copy.wait_recv()
        wide = lax.broadcasted_iota(jnp.int32, (ny, nz), 1)
        joined[slot] = jnp.where(lax.rem(wide, 2) == 0, take[slot, 1], take[slot, 0])

    def add_columns(slot, k, r, value):
        at = pl.ds(r, chunk)
        pack[slot, at, :] = jnp.where(pair_of == k, pltpu.roll(value, 2 * k, 1), pack[slot, at, :])

    def spanwise(slot, k, r, value):
        edge = pltpu.roll(joined[slot, pl.ds(r, chunk), :], lax.rem(nz - 2 * k, nz), 1)
        above = pltpu.roll(jnp.where(lane == 0, edge, value), nz - 1, 1)
        below = pltpu.roll(jnp.where(lane == nz - 1, edge, value), 1, 1)
        return above, below

    loads[0].wait()
    loads[1].wait()

    @pl.loop(0, nx)
    def _(x):
        for r in range(0, ny, chunk):
            at = pl.ds(PAD + r, chunk)
            for c in range(comps):
                add_columns(0, c * nx + x, r, lam[c, x + 1, at, :])
            add_columns(0, comps * nx + x, r, visc[x + 1, at, :])

    for copy in columns(0):
        copy.start()

    block_rows = ny // BY
    part = gate.shape[1]

    @pl.when(gx == 0)
    def _():
        lists = lists_ref[pl.ds(pl.multiple_of(gz * block_rows, block_rows), block_rows), :]
        tile_id = lax.broadcasted_iota(jnp.int32, (block_rows, tiles), 1)
        named = jnp.zeros((block_rows, tiles), f32)
        for l in range(lists.shape[1]):
            named = named + jnp.where(lists[:, l:l + 1] == tile_id, 1.0, 0.0)
        spread = (lax.broadcasted_iota(jnp.int32, (ny, block_rows), 0) // BY
                  == lax.broadcasted_iota(jnp.int32, (ny, block_rows), 1))
        named = jnp.dot(jnp.where(spread, 1.0, 0.0).astype(jnp.bfloat16), named.astype(jnp.bfloat16),
                        preferred_element_type=f32).astype(jnp.bfloat16)
        same_row = (lax.rem(lax.broadcasted_iota(jnp.int32, (part, ny), 0), BY)
                    == lax.rem(lax.broadcasted_iota(jnp.int32, (part, ny), 1), BY))

        @pl.loop(0, gate.shape[0])
        def _(j):
            wanted = (lax.broadcasted_iota(jnp.int32, (part, tiles), 0) + j * part) // BY
            moved = jnp.where(place_ref[...] == wanted, 1.0, 0.0).astype(jnp.bfloat16)
            chosen = lax.dot_general(moved, named, (((1,), (1,)), ((), ())), preferred_element_type=f32)
            gate[j] = jnp.where(same_row, chosen, 0.0).astype(jnp.bfloat16)

    loads[2].wait()
    await_layers(visc_layers)
    await_layers(lam_layers)
    join(0)

    def first_step(x, slot, k_of):
        for r in range(0, ny, chunk):
            at = pl.ds(PAD + r, chunk)
            plain = pl.ds(r, chunk)
            v = visc[x + 1, at, :]
            v_above, v_below = spanwise(0, comps * nx + x, r, v)
            faces = [0.5 * (v + other) for other in (
                visc[x + 2, at, :], visc[x, at, :],
                visc[x + 1, pl.ds(PAD + r + 1, chunk), :], visc[x + 1, pl.ds(PAD + r - 1, chunk), :],
                v_above, v_below)]
            total = ((faces[0] + faces[1]) + (faces[2] + faces[3])) + (faces[4] + faces[5])
            weights = []
            for d in range(3):
                speed = 0.5 * vel[d, x, plain, :]
                weights += [faces[2 * d] + speed, faces[2 * d + 1] - speed]
            weights.append(1.0 - total)
            for n, weight in enumerate(weights):
                coef[n, x, plain, :] = weight
            for c in range(comps):
                value = combine(lam, 0, c * nx + x, c, x, r, weights)
                mid[c, x + 1, at, :] = value
                add_columns(slot, k_of(c), r, value)

    def combine(field, slot, k, c, x, r, weights):
        at = pl.ds(PAD + r, chunk)
        centre = field[c, x + 1, at, :]
        above, below = spanwise(slot, k, r, centre)
        result = weights[6] * centre + weights[4] * above + weights[5] * below
        result = result + weights[0] * field[c, x + 2, at, :] + weights[1] * field[c, x, at, :]
        result = result + weights[2] * field[c, x + 1, pl.ds(PAD + r + 1, chunk), :]
        return result + weights[3] * field[c, x + 1, pl.ds(PAD + r - 1, chunk), :]

    first_step(0, 1, lambda c: c * half)
    first_step(nx - 1, 2, lambda c: c * half + half - 1)
    start_layers(mid_layers)

    @pl.loop(1, half)
    def _(x):
        first_step(x, 1, lambda c: c * half + x)

    for copy in columns(1):
        copy.start()

    @pl.loop(half, nx - 1)
    def _(x):
        first_step(x, 2, lambda c: c * half + x - half)

    for copy in columns(2):
        copy.start()

    def store(x):
        return pltpu.make_async_copy(out.at[:, x], out_hbm.at[:, x], store_sem.at[x])

    def second_step(x, slot, first):
        for r in range(0, ny, chunk):
            plain = pl.ds(r, chunk)
            weights = [coef[n, x, plain, :] for n in range(7)]
            for c in range(comps):
                out[c, x, plain, :] = combine(mid, slot, c * half + x - first, c, x, r, weights)
        store(x).start()

    join(1)
    await_layers(mid_layers)
    second_step(0, 1, 0)

    def tile_copy(d, source):
        return pltpu.make_async_remote_copy(
            contrib.at[d], got.at[source], t_send.at[d], t_recv.at[source],
            device_id=(d // gzn, lax.rem(d, gzn)), device_id_type=MESH)

    @pl.when(gx == 0)
    def _():
        owners = part // (tile_rows * BY)
        for c in range(comps):
            high, low = split_parts(out[c, 0])
            both = jnp.concatenate([high, low], axis=1)

            @pl.loop(0, gate.shape[0])
            def _(j):
                sums = jnp.dot(gate[j], both, preferred_element_type=f32)
                sums = sums[:, :nz] + sums[:, nz:]
                contrib[pl.ds(j * owners, owners), :, c * nz:(c + 1) * nz] = sums.reshape(
                    owners, tile_rows * BY, nz)

        got[gz] = contrib[me]

        @pl.loop(0, gxn * gzn)
        def _(d):
            @pl.when(d != me)
            def _():
                tile_copy(d, gz).start()

    @pl.loop(1, half)
    def _(x):
        second_step(x, 1, 0)

    join(2)

    @pl.loop(half, nx)
    def _(x):
        second_step(x, 2, half)

    for s in range(gzn):
        @pl.when((gx > 0) | (gz != s))
        def _():
            tile_copy(me, s).wait_recv()

    loads[3].wait()
    sums = got[0]
    for s in range(1, gzn):
        sums = sums + got[s]
    left_side[...] = jnp.zeros_like(left_side)
    for t in range(tile_rows):
        for c in range(comps):
            for i in range(BY):
                left_side[t, c:c + 1, i * nz:(i + 1) * nz] = sums[
                    t * BY + i:t * BY + i + 1, c * nz:(c + 1) * nz]
    for t in range(tile_rows):
        high, low = split_parts(left_side[t])
        product = (jnp.dot(high, filt[t], preferred_element_type=f32)
                   + jnp.dot(low, filt[t], preferred_element_type=f32))
        grad_ref[t] = product[:comps]

    for pair in (visc_layers, lam_layers, mid_layers):
        await_sent(pair)
    for slot in range(3):
        for copy in columns(slot):
            copy.wait_send()

    @pl.when(gx == 0)
    def _():
        @pl.loop(0, gxn * gzn)
        def _(d):
            @pl.when(d != me)
            def _():
                tile_copy(d, gz).wait_send()

    @pl.loop(0, nx)
    def _(x):
        store(x).wait()


def shards(adjoint, velocity, viscosity, filters, block_tiles, tile_place):
    gxn, gzn = lax.axis_size("gx"), lax.axis_size("gz")
    comps, nx, ny, nz = adjoint.shape
    tile_rows, order, _ = filters.shape
    tiles = tile_place.shape[0]
    devices = gxn * gzn
    part = min(512, tiles * BY)
    f32 = jnp.float32
    padded = (nx + 2, ny + 2 * PAD, nz)
    anywhere = pl.BlockSpec(memory_space=pl.ANY)
    vmem = pl.BlockSpec(memory_space=pltpu.VMEM)
    dma = pltpu.SemaphoreType.DMA
    return pl.pallas_call(
        functools.partial(kernel, gxn, gzn, 32),
        out_shape=(
            jax.ShapeDtypeStruct(adjoint.shape, f32),
            jax.ShapeDtypeStruct((tile_rows, comps, order), f32),
        ),
        in_specs=[anywhere] * 4 + [vmem] * 2,
        out_specs=(anywhere, vmem),
        scratch_shapes=[
            pltpu.VMEM((comps,) + padded, f32),
            pltpu.VMEM((comps,) + padded, f32),
            pltpu.VMEM(padded, f32),
            pltpu.VMEM(velocity.shape, f32),
            pltpu.VMEM(filters.shape, filters.dtype),
            pltpu.VMEM((7, nx, ny, nz), f32),
            pltpu.VMEM(adjoint.shape, f32),
            pltpu.VMEM((3, ny, nz), f32),
            pltpu.VMEM((3, 2, ny, nz), f32),
            pltpu.VMEM((3, ny, nz), f32),
            pltpu.VMEM((tiles * BY // part, part, ny), jnp.bfloat16),
            pltpu.VMEM((devices, tile_rows * BY, comps * nz), f32),
            pltpu.VMEM((gzn, tile_rows * BY, comps * nz), f32),
            pltpu.VMEM((tile_rows, 8, order), f32),
            dma((4,)),
            dma((nx,)),
            dma((6,)),
            dma((6,)),
            dma((6,)),
            dma((6,)),
            dma((devices,)),
            dma((gzn,)),
        ],
        compiler_params=pltpu.CompilerParams(
            collective_id=0, has_side_effects=True, vmem_limit_bytes=48 * 1024 * 1024
        ),
    )(adjoint, velocity, viscosity, filters, block_tiles, tile_place[None, :])


def solution(mesh):
    placed = (
        P(None, "gx", None, "gz"),
        P(None, "gx", None, "gz"),
        P("gx", None, "gz"),
        P(("gx", "gz"), None, None),
        P(),
        P(),
    )
    return jax.shard_map(
        shards,
        mesh=mesh,
        in_specs=placed,
        out_specs=(P(None, "gx", None, "gz"), P(("gx", "gz"), None, None)),
        check_vma=False,
    )
```

time: 315 us -> 46.6 us (0.15)
  the two profiles are of different devices: /device:TPU:0 before, /device:TPU:7 now
where the time goes in v1:
time: 46.6 us; the launch traced here: 46.4 us
  Pallas kernels  37 us (79%)
  local copies, waits for them, and re-layouts  8.78 us (19%)
  between operations  0.65 us (1%)
    pallas_call x1, Pallas kernels, shards(): pl.pallas_call(functools.partial(kernel, gxn, gzn, 32), out_shape=(jax.Sh...  37 us
    unnamed x8, local copies, waits for them, and re-layouts  8.16 us

profile of v1, /device:TPU:7, one launch (start us, length us, event | category | flops | bytes accessed | tf_op | source)
XLA Modules:
  0.0 46.4 jit_solution(8660615359451618324)
XLA Ops:
  0.6 0.8 %copy.8.lists_ref = s32[128,8]{1,0:T(8,128)S(1)} copy(s32[128,8]{0,1:T(8,128)} %param.10) | data formatting | bytes 8192 | tf_op args[4]
  1.4 0.0 copy-start
  1.4 1.6 %copy-done = bf16[4,512,512]{2,1,0:T(8,128)(2,1)S(1)} copy-done((bf16[4,512,512]{2,1,0:T(8,128)(2,1)S(1)}, bf16[4,512,512]{2,1,0:T(8,128)(2,1)}, u32[]{:S(2)}) %copy-start) | copy-done | bytes 2097176
  3.0 0.0 copy-start.1
  3.0 1.2 %copy-done.1 = f32[16,128,128]{2,1,0:T(8,128)S(1)} copy-done((f32[16,128,128]{2,1,0:T(8,128)S(1)}, f32[16,128,128]{2,1,0:T(8,128)}, u32[]{:S(2)}) %copy-start.1) | copy-done | bytes 1048600
  4.2 0.0 copy-start.2
  4.2 0.7 %copy-done.2 = s32[128]{0:T(128)S(1)} copy-done((s32[128]{0:T(128)S(1)}, s32[128]{0:T(128)}, u32[]{:S(2)}) %copy-start.2) | copy-done | bytes 536
  4.9 37.0 %shard_map.77 = (f32[3,16,128,128]{3,2,1,0:T(8,128)}, f32[4,3,512]{2,1,0:T(4,128)S(1)}) custom-call(f32[3,16,128,128]{3,2,1,0:T(8,128)} %adj_hbm.1, f32[3,16,128,128]{3,2,1,0:T(8,128)} %vel_hbm.1, f32[16,128,128]{2,1,0:T(8,128)S(1)} %copy-done.1, bf16[4,512,512]{2,1,0:T(8,128)(2,1)S(1)} %copy-done, s32[128,8]{1,0:T(8,128)S(1)} %copy.8.lists_ref, ...), custom_call_target="tpu_custom_call" | custom-call | tf_op jit(solution)/shard_map/pallas_call | solution.py:375
  41.9 0.6 %copy.9 = f32[4,3,512]{2,0,1:T(4,128)} copy(f32[4,3,512]{2,1,0:T(4,128)S(1)} %get-tuple-element.3) | data formatting | bytes 49152 | tf_op jit(solution)/shard_map/pallas_call | solution.py:375
  42.5 3.9 %copy.11 = f32[3,16,128,128]{3,2,1,0:T(8,128)} copy(f32[3,16,128,128]{3,2,1,0:T(8,128)} %get-tuple-element.6) | data formatting | bytes 6291456
Async XLA Ops:
  1.4 1.6 %copy-start = (bf16[4,512,512]{2,1,0:T(8,128)(2,1)S(1)}, bf16[4,512,512]{2,1,0:T(8,128)(2,1)}, u32[]{:S(2)}) copy-start(bf16[4,512,512]{2,1,0:T(8,128)(2,1)} %filt_hbm.1) | copy-start | bytes 6291460
  3.0 1.2 %copy-start.1 = (f32[16,128,128]{2,1,0:T(8,128)S(1)}, f32[16,128,128]{2,1,0:T(8,128)}, u32[]{:S(2)}) copy-start(f32[16,128,128]{2,1,0:T(8,128)} %visc_hbm.1) | copy-start | bytes 3145732
  4.2 0.7 %copy-start.2 = (s32[128]{0:T(128)S(1)}, s32[128]{0:T(128)}, u32[]{:S(2)}) copy-start(s32[128]{0:T(128)} %param.11) | copy-start | bytes 1540

commit v2 on v1

--- a/solution.py
+++ b/solution.py
@@ -28,7 +28,9 @@
     comps, nx, ny, nz = adj_hbm.shape
     tiles = place_ref.shape[1]
     tile_rows = filt_hbm.shape[0]
-    half = nx // 2
+    early = 3 * nx // 8
+    face_at = nx // 2 + 1
+    late = nx - early
     gx = lax.axis_index("gx")
     gz = lax.axis_index("gz")
     upper = lax.rem(gz + 1, gzn)
@@ -250,38 +252,35 @@
         result = result + weights[2] * field[c, x + 1, pl.ds(PAD + r + 1, chunk), :]
         return result + weights[3] * field[c, x + 1, pl.ds(PAD + r - 1, chunk), :]
 
-    first_step(0, 1, lambda c: c * half)
-    first_step(nx - 1, 2, lambda c: c * half + half - 1)
+    first_step(0, 1, lambda c: c * early)
+    first_step(nx - 1, 2, lambda c: c * late + late - 1)
     start_layers(mid_layers)
 
-    @pl.loop(1, half)
-    def _(x):
-        first_step(x, 1, lambda c: c * half + x)
+    @pl.loop(1, early)
+    def _(x):
+        first_step(x, 1, lambda c: c * early + x)
 
     for copy in columns(1):
         copy.start()
 
-    @pl.loop(half, nx - 1)
-    def _(x):
-        first_step(x, 2, lambda c: c * half + x - half)
-
-    for copy in columns(2):
-        copy.start()
+    @pl.loop(early, face_at)
+    def _(x):
+        first_step(x, 2, lambda c: c * late + x - early)
 
     def store(x):
         return pltpu.make_async_copy(out.at[:, x], out_hbm.at[:, x], store_sem.at[x])
 
-    def second_step(x, slot, first):
+    def second_step(x, slot, first, count):
         for r in range(0, ny, chunk):
             plain = pl.ds(r, chunk)
             weights = [coef[n, x, plain, :] for n in range(7)]
             for c in range(comps):
-                out[c, x, plain, :] = combine(mid, slot, c * half + x - first, c, x, r, weights)
+                out[c, x, plain, :] = combine(mid, slot, c * count + x - first, c, x, r, weights)
         store(x).start()
 
     join(1)
     await_layers(mid_layers)
-    second_step(0, 1, 0)
+    second_step(0, 1, 0, early)
 
     def tile_copy(d, source):
         return pltpu.make_async_remote_copy(
@@ -310,15 +309,22 @@
             def _():
                 tile_copy(d, gz).start()
 
-    @pl.loop(1, half)
-    def _(x):
-        second_step(x, 1, 0)
+    @pl.loop(face_at, nx - 1)
+    def _(x):
+        first_step(x, 2, lambda c: c * late + x - early)
+
+    for copy in columns(2):
+        copy.start()
+
+    @pl.loop(1, early)
+    def _(x):
+        second_step(x, 1, 0, early)
 
     join(2)
 
-    @pl.loop(half, nx)
-    def _(x):
-        second_step(x, 2, half)
+    @pl.loop(early, nx)
+    def _(x):
+        second_step(x, 2, early, late)
 
     for s in range(gzn):
         @pl.when((gx > 0) | (gz != s))
@@ -360,6 +366,17 @@
         store(x).wait()
 
 
+def move(source, target, sem):
+    copies = [
+        pltpu.make_async_copy(source.at[c, pl.ds(x, 4)], target.at[c, pl.ds(x, 4)], sem.at[c, x // 4])
+        for c in range(source.shape[0]) for x in range(0, source.shape[1], 4)
+    ]
+    for copy in copies:
+        copy.start()
+    for copy in copies:
+        copy.wait()
+
+
 def shards(adjoint, velocity, viscosity, filters, block_tiles, tile_place):
     gxn, gzn = lax.axis_size("gx"), lax.axis_size("gz")
     comps, nx, ny, nz = adjoint.shape
@@ -372,7 +389,7 @@
     anywhere = pl.BlockSpec(memory_space=pl.ANY)
     vmem = pl.BlockSpec(memory_space=pltpu.VMEM)
     dma = pltpu.SemaphoreType.DMA
-    return pl.pallas_call(
+    field, gradient = pl.pallas_call(
         functools.partial(kernel, gxn, gzn, 32),
         out_shape=(
             jax.ShapeDtypeStruct(adjoint.shape, f32),
@@ -405,9 +422,18 @@
             dma((gzn,)),
         ],
         compiler_params=pltpu.CompilerParams(
-            collective_id=0, has_side_effects=True, vmem_limit_bytes=48 * 1024 * 1024
+            collective_id=0, has_side_effects=True, vmem_limit_bytes=62 * 1024 * 1024
         ),
     )(adjoint, velocity, viscosity, filters, block_tiles, tile_place[None, :])
+    field = pl.pallas_call(
+        move,
+        out_shape=jax.ShapeDtypeStruct(field.shape, f32),
+        in_specs=[anywhere],
+        out_specs=anywhere,
+        scratch_shapes=[dma((comps, nx // 4))],
+        compiler_params=pltpu.CompilerParams(vmem_limit_bytes=62 * 1024 * 1024),
+    )(field)
+    return field, gradient
 
 
 def solution(mesh):

time: 46.6 us -> 142 us (3.05)
  the two profiles are of different devices: /device:TPU:7 before, /device:TPU:0 now
where the time goes in v2:
time: 142 us
  Pallas kernels  139 us (98%)
  local copies, waits for them, and re-layouts  2.04 us (1%)
    pallas_call x1, Pallas kernels, shards(): pl.pallas_call(move, out_shape=jax.ShapeDtypeStruct(field.shape, f32), in...  96.5 us
    pallas_call x1, Pallas kernels, shards(): pl.pallas_call(functools.partial(kernel, gxn, gzn, 32), out_shape=(jax.Sh...  42.6 us

profile of v2, /device:TPU:0, one launch (start us, length us, event | category | flops | bytes accessed | tf_op | source)
XLA Modules:
  0.0 141.8 jit_solution(6292119469659373994)
XLA Ops:
  0.6 1.4 copy.8.lists_ref
  2.0 42.6 %shard_map.77 = (f32[3,16,128,128]{3,2,1,0:T(8,128)}, f32[4,3,512]{2,1,0:T(4,128)}) custom-call(f32[3,16,128,128]{3,2,1,0:T(8,128)} %adj_hbm.1, f32[3,16,128,128]{3,2,1,0:T(8,128)} %vel_hbm.1, f32[16,128,128]{2,1,0:T(8,128)} %visc_hbm.1, bf16[4,512,512]{2,1,0:T(8,128)(2,1)} %filt_hbm.1, s32[128,8]{1,0:T(8,128)} %copy.8.lists_ref, s32[1,128]{1,0:T(1,128)} %bitcast.1), custom_call_target="tpu_custom_call" | custom-call | tf_op jit(solution)/shard_map/pallas_call | solution.py:392
  44.7 0.0 copy-start
  44.7 96.5 %shard_map.78 = f32[3,16,128,128]{3,2,1,0:T(8,128)} custom-call(f32[3,16,128,128]{3,2,1,0:T(8,128)} %get-tuple-element.4.source), custom_call_target="tpu_custom_call" | custom-call | tf_op jit(solution)/shard_map/pallas_call | solution.py:428
  141.2 0.0 copy-done
  141.2 0.6 copy.9
Async XLA Ops:
  44.7 96.5 %copy-start = (f32[4,3,512]{2,1,0:T(4,128)S(1)}, f32[4,3,512]{2,1,0:T(4,128)}, u32[]{:S(2)}) copy-start(f32[4,3,512]{2,1,0:T(4,128)} %get-tuple-element.7) | copy-start | bytes 73732
